TPU v7x, 256 devices: a whole 4x4x8 slice. The times are simulated.
256 devices in a mesh: ctx: 8 (over x, core), exp: 16 (over y_hi, z), dp: 2 (over y_lo).
Axes of the slice: x: 4, y: 4 (y_hi: 2, y_lo: 2; y = y_hi * 2 + y_lo), z: 8, core: 2. Of those that a mesh axis runs over, the one named last changes fastest.
Arguments:
- hidden_in: bfloat16 [32768, 3584], P(('dp', 'ctx', 'exp')), parts along dimension 0, may hold values from -6 to 6
- queries: bfloat16 [32768, 3584], P(('dp', 'ctx', 'exp')), parts along dimension 0, may hold values from -6 to 6
- keys_values: bfloat16 [32768, 1024], P(('dp', 'ctx', 'exp')), parts along dimension 0, may hold values from -6 to 6
- doc_ids: int32 [32768], P(('dp', 'ctx', 'exp')), parts along dimension 0, may hold values from 0 to 15, never falling along the last dimension, each value on 1 to 2048 neighbouring positions
- route_ids: int32 [32768, 8], P(('dp', 'ctx', 'exp')), parts along dimension 0, may hold values from 0 to 63, as said below
- route_weights: float32 [32768, 8], P(('dp', 'ctx', 'exp')), parts along dimension 0, may hold values from 0.1 to 0.6
- norm_gain: bfloat16 [3584], replicated, may hold values from 0.5 to 1.5
- gate_up: bfloat16 [2, 2, 3584, 2560], P(None, None, None, 'exp'), may hold values from -0.09375 to 0.09375
- down: bfloat16 [2, 2560, 3584], P(None, 'exp'), may hold values from -0.125 to 0.125
Outputs:
- output: bfloat16 [32768, 3584], P(('dp', 'ctx', 'exp')), parts along dimension 0
There are 2 independent parts, one for each index of `dp`. A program takes and returns all parts, laid end to end along the dimension named above; an argument that names none is the same for every part. Nothing has to cross between parts.
Inputs may be any that keep to these rules, and one draw needn't show every extreme that they name: `doc_ids`: each document is a run of consecutive tokens of at most 2048 tokens; ids never fall along the sequence. `route_ids`: the ids in a row are distinct; within the 128 rows of one device (aligned blocks), each expert below 2 is named by at most 32 rows, and by exactly 32 rows in some block.
All inputs are finite; a program needn't handle non-finite values.
Results may differ from a plain program's by a relative error of at most 0.009.
Values may be sent and summed in bfloat16 or wider, within the bound.
No kernel may reach another device: no remote copies, remote signals or barrier semaphores. Data moves between devices by JAX's collectives and lax.ppermute only.
A program may use at most 128 MiB of HBM per device.

v0:
```python
import jax
import jax.numpy as jnp
from jax import lax
from jax.sharding import PartitionSpec as P

HEADS = 28
KV_HEADS = 4
HEAD_DIM = 128
EXP_FLIGHT = 2


def from_behind(value, axis, steps):
    count = lax.axis_size(axis)
    initial, last = (max(0, -steps), min(count, count - steps))
    return lax.ppermute(value, axis, [(source, source + steps) for source in range(initial, last)])


def expert_terms(segment, gate_up_part, down_part, flights, capacity):
    stacks = segment.shape[0] // (flights * capacity)
    shaped = segment.reshape(stacks, flights, capacity, segment.shape[1])
    gate_part = jnp.einsum(
        "necd,edf->necf", shaped, gate_up_part[:, 0], preferred_element_type=jnp.float32
    )
    up_part = jnp.einsum(
        "necd,edf->necf", shaped, gate_up_part[:, 1], preferred_element_type=jnp.float32
    )
    hidden_act = (jax.nn.silu(gate_part) * up_part).astype(jnp.bfloat16)
    result = jnp.einsum("necf,efd->necd", hidden_act, down_part, preferred_element_type=jnp.float32)
    return result.reshape(segment.shape[0], down_part.shape[2])


def body(
    hidden_in, queries, keys_values, doc_ids, route_ids, route_weights, norm_gain, gate_up, down
):
    tok_rows = queries.shape[0]
    slab_len = tok_rows * lax.axis_size("exp")
    ctx_index = lax.axis_index("ctx")
    exp_index = lax.axis_index("exp")
    own_kv, own_doc = (
        lax.all_gather(keys_values, "exp", axis=0, tiled=True),
        lax.all_gather(doc_ids, "exp", axis=0, tiled=True),
    )
    prior_kv, prior_doc = from_behind((own_kv, own_doc), "ctx", 1)
    key_span = min(512, slab_len)
    span_count = -(-(slab_len + tok_rows) // key_span)
    all_kv = jnp.concatenate(
        [prior_kv, own_kv, jnp.zeros((key_span, own_kv.shape[1]), own_kv.dtype)], 0
    )
    all_doc = jnp.concatenate([prior_doc, own_doc, jnp.full((key_span,), -1, jnp.int32)], 0)
    q_group = HEADS // KV_HEADS
    kv_width = KV_HEADS * HEAD_DIM
    score_scale = HEAD_DIM ** (-0.5)
    shaped_q = queries.reshape(tok_rows, KV_HEADS, q_group, HEAD_DIM)
    query_pos = ctx_index * slab_len + exp_index * tok_rows + jnp.arange(tok_rows, dtype=jnp.int32)
    key_base = (ctx_index - 1) * slab_len
    first_key = exp_index * tok_rows

    def one_span(span_index, state_tuple):
        running, totals, weighted = state_tuple
        offset = first_key + span_index * key_span
        key_block = lax.dynamic_slice_in_dim(all_kv, offset, key_span, 0)
        block_doc = lax.dynamic_slice_in_dim(all_doc, offset, key_span, 0)
        key_pos = key_base + offset + jnp.arange(key_span, dtype=jnp.int32)
        allowed = (
            (doc_ids[:, None] == block_doc[None, :])
            & (key_pos[None, :] <= query_pos[:, None])
            & (key_pos[None, :] >= 0)
        )
        key_rows = key_block[:, :kv_width].reshape(key_span, KV_HEADS, HEAD_DIM)
        value_rows = key_block[:, kv_width:].reshape(key_span, KV_HEADS, HEAD_DIM)
        scores = (
            jnp.einsum("tkgd,skd->kgts", shaped_q, key_rows, preferred_element_type=jnp.float32)
            * score_scale
        )
        scores = jnp.where(allowed, scores, -1e30)
        new_running = jnp.maximum(running, jnp.max(scores, axis=-1))
        powers = jnp.where(allowed, jnp.exp(scores - new_running[..., None]), 0.0)
        shrink = jnp.exp(running - new_running)
        totals = totals * shrink + jnp.sum(powers, axis=-1)
        weighted = weighted * shrink[..., None] + jnp.einsum(
            "kgts,skd->kgtd",
            powers.astype(jnp.bfloat16),
            value_rows,
            preferred_element_type=jnp.float32,
        )
        return (new_running, totals, weighted)

    start_state = (
        jnp.full((KV_HEADS, q_group, tok_rows), -1e30, jnp.float32),
        jnp.zeros((KV_HEADS, q_group, tok_rows), jnp.float32),
        jnp.zeros((KV_HEADS, q_group, tok_rows, HEAD_DIM), jnp.float32),
    )
    running, totals, weighted = lax.fori_loop(0, span_count, one_span, start_state)
    mixture = weighted / totals[..., None]
    attended = (
        jnp.transpose(mixture, (2, 0, 1, 3))
        .reshape(tok_rows, HEADS * HEAD_DIM)
        .astype(jnp.bfloat16)
    )
    stream = (hidden_in.astype(jnp.float32) + attended.astype(jnp.float32)).astype(jnp.bfloat16)
    stream_f = lax.optimization_barrier(stream).astype(jnp.float32)
    inverse = lax.rsqrt(jnp.mean(stream_f * stream_f, axis=-1, keepdims=True) + 1e-06)
    normed = (stream_f * inverse * norm_gain.astype(jnp.float32)).astype(jnp.bfloat16)
    capacity = tok_rows // 4
    slot_ids = jnp.arange(capacity, dtype=jnp.int32)
    panel_list = []
    slot_list = []
    factor_list = []
    for flight in range(EXP_FLIGHT):
        chosen = route_ids == flight
        routed = jnp.any(chosen, axis=1)
        weight = jnp.sum(jnp.where(chosen, route_weights, 0.0), axis=1)
        slot_of = jnp.cumsum(routed.astype(jnp.int32)) - 1
        placing = (slot_of[None, :] == slot_ids[:, None]) & routed[None, :]
        panel_list.append(
            jnp.dot(
                placing.astype(jnp.bfloat16), normed, preferred_element_type=jnp.float32
            ).astype(jnp.bfloat16)
        )
        slot_list.append(jnp.clip(slot_of, 0, capacity - 1))
        factor_list.append(jnp.where(routed, weight, 0.0))
    panels = jnp.concatenate(panel_list, 0)
    gathered = lax.all_gather(panels, "exp", axis=0, tiled=True)
    summed = lax.psum_scatter(
        expert_terms(gathered, gate_up, down, EXP_FLIGHT, capacity).astype(jnp.bfloat16),
        "exp",
        scatter_dimension=0,
        tiled=True,
    ).astype(jnp.float32)
    outputs = [summed[flight * capacity : (flight + 1) * capacity] for flight in range(EXP_FLIGHT)]
    combined = jnp.zeros((tok_rows, hidden_in.shape[1]), jnp.float32)
    for flight in range(EXP_FLIGHT):
        combined = (
            combined
            + jnp.take(outputs[flight], slot_list[flight], axis=0) * factor_list[flight][:, None]
        )
    return (stream_f + combined).astype(jnp.bfloat16)


def solution(mesh):
    in_specs = (
        P(("dp", "ctx", "exp"), None),
        P(("dp", "ctx", "exp"), None),
        P(("dp", "ctx", "exp"), None),
        P(("dp", "ctx", "exp")),
        P(("dp", "ctx", "exp"), None),
        P(("dp", "ctx", "exp"), None),
        P(),
        P(None, None, None, "exp"),
        P(None, "exp", None),
    )
    out_specs = P(("dp", "ctx", "exp"), None)
    return jax.shard_map(body, mesh=mesh, in_specs=in_specs, out_specs=out_specs, check_vma=False)
```

profile of v0, /device:TPU:4, one launch (start us, length us, event | category | flops | bytes accessed | tf_op | source)
XLA Modules:
  0.0 659.9 jit_solution(5113733862659377982)
XLA Ops:
  8.6 109.6 %all-gather.4.cloned.1.call-done = bf16[2048,1024]{0,1:T(8,128)(2,1)} async-done(((bf16[128,1024]{0,1:T(8,128)(2,1)}), bf16[2048,1024]{0,1:T(8,128)(2,1)}) %all-gather.4.cloned.1.call-update) | async-done | bytes 4194320 | tf_op jit(solution)/shard_map/all_gather | solution.py:40
  120.0 38.2 %all-gather = s32[16,1,128]{2,1,0:T(1,128)S(1)} all-gather(s32[1,1,128]{2,1,0:T(1,128)} %bitcast.104), channel_id=1, replica_groups=mesh['ctx'=8,'exp'=16,'dp'=2] {'exp'}, dimensions={0}, use_global_device_ids=true | all-gather | bytes 8704 | tf_op jit(solution)/shard_map/all_gather | solution.py:41
  161.8 2.2 copy.33
  165.7 2.6 collective-permute-done
  168.3 9.1 %maximum_maximum_fusion = bf16[4608,1024]{0,1:T(8,128)(2,1)} fusion(bf16[2048,1024]{0,1:T(8,128)(2,1)} %all-gather.4.cloned.1.call-done, bf16[2048,1024]{0,1:T(8,128)(2,1)} %collective-permute-done.1, bf16[4608]{0:T(1024)(128)(2,1)S(1)} %pad.4.clone), kind=kLoop, calls=%fused_computation.24 | loop fusion | flops 28311552 | bytes 17835008 | tf_op jit(solution)/shard_map/concatenate | solution.py:46
  177.4 85.9 %while.18 = (s32[]{:T(128)}, f32[4,7,128]{2,1,0:T(8,128)S(1)}, f32[4,7,128]{2,1,0:T(8,128)S(1)}, f32[4,7,128,128]{3,2,1,0:T(8,128)}, s32[128]{0:T(128)S(1)}, /*i...) while((s32[]{:T(128)}, f32[4,7,128]{2,1,0:T(8,128)S(1)}, ...), condition=%wide.region_3.4_spmd.clone, body=%wide.region_0.3_spmd.clone.sunk | while | flops 965037184 | bytes 59618084 | solution.py:93
  179.8 4.2 fusion.91
  184.0 5.0 fusion.92
  189.2 4.8 fusion.94
  196.5 4.2 fusion.91
  200.7 5.0 fusion.92
  205.9 5.5 fusion.94
  213.8 4.2 fusion.91
  218.0 5.0 fusion.92
  223.2 5.5 fusion.94
  231.1 4.2 fusion.91
  235.4 5.0 fusion.92
  240.5 5.5 fusion.94
  248.4 4.2 fusion.91
  252.7 5.0 fusion.92
  257.8 5.5 fusion.94
  263.3 2.8 copy.35
  266.1 3.0 fusion.59
  269.1 2.8 copy.36
  276.0 122.0 %all-gather.6.cloned.1.call-done = bf16[1024,3584]{1,0:T(8,128)(2,1)} async-done(((bf16[64,3584]{1,0:T(8,128)(2,1)}), bf16[1024,3584]{1,0:T(8,128)(2,1)}) %all-gather.6.cloned.1.call-update) | async-done | bytes 7340048 | tf_op jit(solution)/shard_map/all_gather | solution.py:123
  398.0 5.8 fusion.30
  403.8 12.2 %fusion.15 = bf16[16,2,32,3584]{3,2,0,1:T(8,128)(2,1)} fusion(bf16[2,160,3584]{2,1,0:T(8,128)(2,1)S(1)} %copy-done, bf16[2,2,3584,160]{2,3,1,0:T(8,128)(2,1)} %param.20, bf16[16,2,32,3584]{3,2,1,0:T(8,128)(2,1)} %bitcast.106, f32[16,2,32,160]{3,2,0,1:T(8,128)S(1)} %fusion.30), kind=kOutput, calls=%fused_computation.26 | convolution fusion | flops 2353463296 | bytes 19922944 | tf_op jit(solution)/shard_map/necf,efd->necd/dot_general | solution.py:28
  416.0 6.8 %copy.43 = bf16[16,2,32,3584]{3,2,1,0:T(8,128)(2,1)} copy(bf16[16,2,32,3584]{3,2,0,1:T(8,128)(2,1)} %fusion.15) | data formatting | bytes 14680064 | tf_op jit(solution)/shard_map/convert_element_type | solution.py:125
  422.9 220.6 %reduce-scatter.2.cloned.1.call-done = bf16[64,3584]{1,0:T(8,128)(2,1)} async-done(((bf16[1024,3584]{1,0:T(8,128)(2,1)}), bf16[64,3584]{1,0:T(8,128)(2,1)}) %reduce-scatter.2.cloned.1.call-update) | async-done | bytes 458768 | tf_op jit(solution)/shard_map/reduce_scatter | solution.py:124
  644.6 2.4 gather_fusion
  647.0 2.4 gather_fusion.1
  649.4 3.9 fusion.28
  (106 shorter events, 27.4 us)
Async XLA Ops:
  6.5 397.2 %copy-start = (bf16[2,160,3584]{2,1,0:T(8,128)(2,1)S(1)}, bf16[2,160,3584]{2,1,0:T(8,128)(2,1)}, u32[]{:S(2)}) copy-start(bf16[2,160,3584]{2,1,0:T(8,128)(2,1)} %param.21) | copy-start | bytes 6881284
  6.5 111.6 %all-gather.4.cloned.1.call-start = ((), (), s32[]{:S(2)}) async-start(), calls=%async_computation.1 | async-start | bytes 4456448 | tf_op jit(solution)/shard_map/all_gather | solution.py:40
  8.5 157.1 %copy-start.5 = (bf16[3584]{0:T(1024)(128)(2,1)S(1)}, bf16[3584]{0:T(1024)(128)(2,1)}, u32[]{:S(2)}) copy-start(bf16[3584]{0:T(1024)(128)(2,1)} %param.19) | copy-start | bytes 21508
  8.5 389.5 %all-gather.6.cloned.1.call-start = ((), (), s32[]{:S(2)}) async-start(), calls=%async_computation.2 | async-start | bytes 7798784 | tf_op jit(solution)/shard_map/all_gather | solution.py:123
  118.1 50.1 %collective-permute-start.1 = (bf16[2048,1024]{0,1:T(8,128)(2,1)}, bf16[2048,1024]{0,1:T(8,128)(2,1)}, u32[]{:S(2)}, u32[]{:S(2)}) collective-permute-start(bf16[2048,1024]{0,1:T(8,128)(2,1)} %all-gather.4.cloned.1.call-done), channel_id=1, source_target_pairs={{0,32},{32,64},{64,96},{96,128},{128,160},{160,192},{192,224},{1,3... | collective-permute-start | bytes 12582920 | tf_op jit(solution)/shard_map/ppermute | solution.py:15
  158.3 10.0 %collective-permute-start = (s32[2048]{0:T(1024)S(1)}, s32[2048]{0:T(1024)S(1)}, u32[]{:S(2)}, u32[]{:S(2)}) collective-permute-start(s32[2048]{0:T(1024)S(1)} %bitcast.102), channel_id=1, source_target_pairs={{0,32},{32,64},{64,96},{96,128},{128,160},{160,192},{192,224},{1,3... | collective-permute-start | bytes 24584 | tf_op jit(solution)/shard_map/ppermute | solution.py:15
  168.3 9.1 %copy-start.4 = (s32[128]{0:T(128)S(1)}, s32[128]{0:T(128)}, u32[]{:S(2)}) copy-start(s32[128]{0:T(128)} %param.16) | copy-start | bytes 1540
  184.0 5.2 copy-start.1
  200.7 5.2 copy-start.1
  218.0 5.2 copy-start.1
  235.4 5.2 copy-start.1
  252.7 5.2 copy-start.1
  269.1 2.8 copy-start.3
  273.6 0.9 copy-start.2
  275.7 367.7 %reduce-scatter.2.cloned.1.call-start = ((), (), s32[]{:S(2)}) async-start(), calls=%async_computation.3 | async-start | bytes 7798784 | tf_op jit(solution)/shard_map/reduce_scatter | solution.py:124
Sparse Core Ops, SparseCore 0:
  9.8 108.2 all-gather.3
  275.9 122.0 all-gather.5
  422.9 220.5 reduce-scatter.1
where the time goes:
time: 661 us; the launch traced here: 660 us
  waiting for transfers between devices  455 us (69%)
  matrix products  66.7 us (10%)
  other arithmetic  46.4 us (7%)
  blocking collectives  38.2 us (6%)
  local copies, waits for them, and re-layouts  36.3 us (5%)
  between operations  13.3 us (2%)
    reduce_scatter x1, waiting for transfers between devices, body(): lax.psum_scatter(expert_terms(gathered, gate_up, down, EXP_FLIGHT, capaci...  221 us
    all_gather x1, waiting for transfers between devices, body(): gathered = lax.all_gather(panels, 'exp', axis=0, tiled=True)  122 us
    all_gather x1, waiting for transfers between devices, body(): lax.all_gather(keys_values, 'exp', axis=0, tiled=True)  110 us
    all_gather x1, blocking collectives, body(): lax.all_gather(doc_ids, 'exp', axis=0, tiled=True)  38.2 us
    dot_general x5, matrix products, one_span(): jnp.einsum('kgts,skd->kgtd', powers.astype(jnp.bfloat16), value_rows, pre...  26.6 us
    reduce_sum x5, other arithmetic, one_span(): totals = totals * shrink + jnp.sum(powers, axis=-1)  24.8 us
    dot_general x5, matrix products, one_span(): jnp.einsum('tkgd,skd->kgts', shaped_q, key_rows, preferred_element_type=j...  21.2 us
  transfers between devices with their start and end apart: 5, of which 4 were waited for; matrix products, arithmetic and copies ran while one was open for 1% of the time, Pallas kernels for 0%

commit v1 on v0

v1 whole, which is shorter than its diff:
```python
import functools
import math

import jax
import jax.numpy as jnp
from jax import lax
from jax.experimental import pallas as pl
from jax.experimental.pallas import tpu as pltpu
from jax.sharding import Mesh
from jax.sharding import PartitionSpec as P

EXP_FLIGHT = 2
HEADS=28; KV_HEADS=4; HD=128; GROUP=7
EXP2_SCALE = math.log2(math.e) / math.sqrt(HD)

def attend_kernel(info_ref, q_ref, hid_ref, start_ref, gain_ref, place_ref, pa_ref, pb_ref, oa_ref, ob_ref,
                  stream_ref, panel_ref, kscr, vscr, m_scr, l_scr, acc_scr, s_all, ssq, sem, *, tok, span):
    c = pl.program_id(0)
    nc = pl.num_programs(0)
    half = oa_ref.shape[0]
    wide = GROUP * HD
    first = info_ref[0]
    off_a = pl.multiple_of(info_ref[1], half)
    off_b = pl.multiple_of(half - info_ref[1], half)
    start_min = info_ref[2]
    start_max = info_ref[3]

    def copies(head, slot):
        out = []
        for n, (src, off) in enumerate(((pa_ref, off_a), (pb_ref, off_b), (oa_ref, off_a + 2 * half), (ob_ref, off_b + 2 * half))):
            for which, dst in ((0, kscr), (1, vscr)):
                col = pl.multiple_of(which * KV_HEADS * HD + head * HD, HD)
                out.append(pltpu.make_async_copy(src.at[:, pl.ds(col, HD)], dst.at[slot, pl.ds(off, half), :], sem.at[slot, n, which]))
        return out

    slot = lax.rem(c, 2)

    @pl.when(c == 0)
    def _():
        for cp in copies(0, 0):
            cp.start()
        ssq[...] = jnp.zeros_like(ssq)

    @pl.when(c + 1 < nc)
    def _():
        for cp in copies(c + 1, 1 - slot):
            cp.start()
    for cp in copies(c, slot):
        cp.wait()

    q = jnp.concatenate([q_ref[:, g * HD:(g + 1) * HD] for g in range(GROUP)], 0)
    start = start_ref[...]
    row = lax.broadcasted_iota(jnp.int32, (tok, 1), 0) + first + 2 * half

    def scores(offset, width):
        k = kscr[slot, pl.ds(offset, width), :]
        return lax.dot_general(q, k, (((1,), (1,)), ((), ())), preferred_element_type=jnp.float32)

    def rowmax(s, width):
        t = s[:, :128]
        for j in range(1, width // 128):
            t = jnp.maximum(t, s[:, j * 128:(j + 1) * 128])
        return jnp.max(t, axis=1, keepdims=True)

    def lanesum(p, width):
        t = p[:, :128]
        for j in range(1, width // 128):
            t = t + p[:, j * 128:(j + 1) * 128]
        return t

    def masked(s, offset, width, causal):
        key = lax.broadcasted_iota(jnp.int32, (tok, width), 1) + offset
        ok = key >= start
        if causal:
            ok = ok & (key <= row)
        return jnp.where(ok[None], s.reshape(GROUP, tok, width), -1e30).reshape(GROUP * tok, width)

    own = pl.multiple_of(first + 2 * half, tok)
    s = masked(scores(own, tok), own, tok, True)
    m = rowmax(s, tok)
    p = jnp.exp2((s - m) * EXP2_SCALE)
    m_scr[...] = jnp.broadcast_to(m, m_scr.shape)
    l_scr[...] = lanesum(p, tok)
    acc_scr[...] = jnp.dot(p.astype(jnp.bfloat16), vscr[slot, pl.ds(own, tok), :], preferred_element_type=jnp.float32)

    def step(i, mask):
        offset = pl.multiple_of(first + i * span, tok)
        s = scores(offset, span)
        if mask:
            s = masked(s, offset, span, False)
        old = m_scr[...]
        new = jnp.maximum(old, rowmax(s, span))
        m_scr[...] = new
        shrink = jnp.exp2((old - new) * EXP2_SCALE)
        p = jnp.exp2((s - jnp.concatenate([new] * (span // 128), 1)) * EXP2_SCALE)
        l_scr[...] = l_scr[...] * shrink + lanesum(p, span)
        acc_scr[...] = acc_scr[...] * shrink + jnp.dot(p.astype(jnp.bfloat16), vscr[slot, pl.ds(offset, span), :], preferred_element_type=jnp.float32)

    count = 2 * half // span
    begin = jnp.clip(lax.div(start_min - first, span), 0, count)

    def loop(i, carry):
        whole = start_max <= first + i * span
        @pl.when(whole)
        def _():
            step(i, False)
        @pl.when(jnp.logical_not(whole))
        def _():
            step(i, True)
        return carry
    lax.fori_loop(begin, count, loop, 0)

    total = jnp.sum(l_scr[...], axis=1, keepdims=True)
    att = (acc_scr[...] / total).astype(jnp.bfloat16).astype(jnp.float32)
    att = jnp.concatenate([att[g * tok:(g + 1) * tok] for g in range(GROUP)], 1)
    stream = (hid_ref[...].astype(jnp.float32) + att).astype(jnp.bfloat16)
    stream_ref[...] = stream
    sf = stream.astype(jnp.float32)
    ssq[...] += lanesum(sf * sf, wide)
    for h in range(KV_HEADS):
        @pl.when(c == h)
        def _(h=h):
            s_all[:, h * wide:(h + 1) * wide] = stream

    @pl.when(c == nc - 1)
    def _():
        inv = lax.rsqrt(jnp.sum(ssq[...], axis=1, keepdims=True) / (KV_HEADS * wide) + 1e-6)
        normed = (s_all[...].astype(jnp.float32) * inv * gain_ref[...].astype(jnp.float32)).astype(jnp.bfloat16)
        panel_ref[...] = jnp.dot(place_ref[...], normed, preferred_element_type=jnp.float32).astype(jnp.bfloat16)

def attend(info, queries, hidden, start, gain, place, pa, pb, oa, ob, span=512):
    tok, d = queries.shape
    wide = GROUP * HD
    half = oa.shape[0]
    rows = place.shape[0]
    blk = pl.BlockSpec((tok, wide), lambda c, s: (0, c))
    whole = lambda shape: pl.BlockSpec(shape, lambda c, s: (0, 0))
    hbm = pl.BlockSpec(memory_space=pl.ANY)
    return pl.pallas_call(
        functools.partial(attend_kernel, tok=tok, span=span),
        grid_spec=pltpu.PrefetchScalarGridSpec(
            num_scalar_prefetch=1, grid=(KV_HEADS,),
            in_specs=[blk, blk, whole((tok, 1)), whole((1, d)), whole((rows, tok)), hbm, hbm, hbm, hbm],
            out_specs=[blk, whole((rows, d))],
            scratch_shapes=[pltpu.VMEM((2, 4 * half, HD), jnp.bfloat16), pltpu.VMEM((2, 4 * half, HD), jnp.bfloat16),
                            pltpu.VMEM((GROUP * tok, 128), jnp.float32), pltpu.VMEM((GROUP * tok, 128), jnp.float32),
                            pltpu.VMEM((GROUP * tok, 128), jnp.float32), pltpu.VMEM((tok, d), jnp.bfloat16),
                            pltpu.VMEM((tok, 128), jnp.float32), pltpu.SemaphoreType.DMA((2, 4, 2))]),
        out_shape=[jax.ShapeDtypeStruct((tok, d), jnp.bfloat16), jax.ShapeDtypeStruct((rows, d), jnp.bfloat16)],
        compiler_params=pltpu.CompilerParams(vmem_limit_bytes=48 << 20),
        cost_estimate=pl.CostEstimate(flops=4 * 10**9, bytes_accessed=12 << 20, transcendentals=8 * 10**6),
        name="attend",
    )(info, queries, hidden, start, gain, place, pa, pb, oa, ob)

def expert_kernel(x_ref, wo_ref, do_ref, r1_ref, r2_ref, y_ref, wg, wu, wd, sem):
    n = wo_ref.shape[1]
    h = r1_ref.shape[1]
    cps = []
    def cp(src, dst):
        c = pltpu.make_async_copy(src, dst, sem.at[len(cps)]); c.start(); cps.append(c)
    cp(wo_ref.at[0], wg.at[pl.ds(0, n)])
    cp(r1_ref.at[0], wg.at[pl.ds(n, h)])
    cp(r2_ref.at[0], wg.at[pl.ds(n + h, h)])
    cp(wo_ref.at[1], wu.at[pl.ds(0, n)])
    cp(r1_ref.at[1], wu.at[pl.ds(n, h)])
    cp(r2_ref.at[1], wu.at[pl.ds(n + h, h)])
    cp(do_ref, wd.at[pl.ds(0, n)])
    cp(r1_ref.at[2], wd.at[pl.ds(n, h)])
    cp(r2_ref.at[2], wd.at[pl.ds(n + h, h)])
    nt = (((1,), (1,)), ((), ()))
    for c in cps[:3]: c.wait()
    x = x_ref[...]
    gate = lax.dot_general(x, wg[...], nt, preferred_element_type=jnp.float32)
    for c in cps[3:6]: c.wait()
    up = lax.dot_general(x, wu[...], nt, preferred_element_type=jnp.float32)
    inner = (gate / (1 + jnp.exp(-gate)) * up).astype(jnp.bfloat16)
    for c in cps[6:]: c.wait()
    y_ref[...] = jnp.dot(inner, wd[...], preferred_element_type=jnp.float32).astype(jnp.bfloat16)

def experts(x, wo, do, r1, r2):
    rows, d = x.shape
    n = wo.shape[1] + r1.shape[1] + r2.shape[1]
    hbm = pl.BlockSpec(memory_space=pl.ANY)
    vm = pl.BlockSpec(memory_space=pltpu.VMEM)
    return pl.pallas_call(
        expert_kernel,
        in_specs=[vm, hbm, hbm, hbm, hbm], out_specs=vm,
        scratch_shapes=[pltpu.VMEM((n, d), jnp.bfloat16)] * 3 + [pltpu.SemaphoreType.DMA((9,))],
        out_shape=jax.ShapeDtypeStruct((rows, d), jnp.bfloat16),
        compiler_params=pltpu.CompilerParams(vmem_limit_bytes=48 << 20),
        cost_estimate=pl.CostEstimate(flops=6 * rows * n * d, bytes_accessed=2 * (3 * n * d + 2 * rows * d), transcendentals=rows * n),
        name="experts",
    )(x, wo, do, r1, r2)


def combine_kernel(stream_ref, keep_ref, back_ref, hot1_ref, hot2_ref, w1_ref, w2_ref, out_ref):
    one = jnp.dot(hot1_ref[...], keep_ref[...], preferred_element_type=jnp.float32)
    two = jnp.dot(hot2_ref[...], back_ref[...], preferred_element_type=jnp.float32)
    total = stream_ref[...].astype(jnp.float32) + one * w1_ref[...] + two * w2_ref[...]
    out_ref[...] = total.astype(out_ref.dtype)


def combine(stream, keep, back, hot1, hot2, w1, w2):
    tok, d = stream.shape
    cap = keep.shape[0]
    wide = d // 4
    cols = lambda rows: pl.BlockSpec((rows, wide), lambda c: (0, c))
    whole = lambda shape: pl.BlockSpec(shape, lambda c: (0, 0))
    return pl.pallas_call(
        combine_kernel,
        grid=(4,),
        in_specs=[cols(tok), cols(cap), cols(cap), whole((tok, cap)), whole((tok, cap)), whole((tok, 1)), whole((tok, 1))],
        out_specs=cols(tok),
        out_shape=jax.ShapeDtypeStruct((tok, d), stream.dtype),
        name="combine",
    )(stream, keep, back, hot1, hot2, w1, w2)


def shift(value, axis, size, steps):
    return lax.ppermute(value, axis, [(i, (i + steps) % size) for i in range(size)])


def swap(value, axis):
    return shift(value, axis, 2, 1)


def doc_starts(doc_ids, sizes):
    ids = jnp.arange(128, dtype=jnp.int32)
    counts = jnp.sum((doc_ids[:, None] < ids[None, :]).astype(jnp.float32), axis=0)
    counts = jnp.broadcast_to(counts[None], (8, 128))
    for axis, size in sizes:
        hop = 1
        while hop < size:
            counts = counts + lax.ppermute(counts, axis, [(i, i ^ hop) for i in range(size)])
            hop *= 2
    hot = doc_ids[:, None] == ids[None, :]
    return jnp.sum(jnp.where(hot, counts[:1], 0.0), axis=1).astype(jnp.int32)


def routing(route_ids, route_weights, flight, capacity):
    chosen = route_ids == flight
    routed = jnp.any(chosen, axis=1)
    weight = jnp.sum(jnp.where(chosen, route_weights, 0.0), axis=1)
    slot_of = jnp.cumsum(routed.astype(jnp.int32)) - 1
    slots = jnp.arange(capacity, dtype=jnp.int32)
    hot = (slot_of[:, None] == slots[None, :]) & routed[:, None]
    return hot.astype(jnp.bfloat16), jnp.where(routed, weight, 0.0)[:, None]


def body(sizes, hidden_in, queries, keys_values, doc_ids, route_ids, route_weights, norm_gain, gate_up, down):
    tok = queries.shape[0]
    capacity = tok // 4
    n_z, n_core, n_cx = sizes["z"], sizes["core"], sizes["cx"]
    yhi, z = lax.axis_index("yhi"), lax.axis_index("z")
    core = lax.axis_index("core")
    ctx = lax.axis_index("cx") * n_core + core
    half = n_z * tok
    n_ctx = n_cx * n_core

    other_kv = swap(keys_values, "yhi")
    own_a = lax.all_gather(keys_values, "z", axis=0, tiled=True)
    own_b = lax.all_gather(other_kv, "z", axis=0, tiled=True)
    ahead = [(i, i + 1) for i in range(n_ctx - 1)]
    prior_a = lax.ppermute(own_a, ("cx", "core"), ahead)
    prior_b = lax.ppermute(own_b, ("cx", "core"), ahead)

    wide_t = jnp.swapaxes(gate_up, 2, 3)
    units = wide_t.shape[2] // n_core
    theirs = jnp.concatenate(
        [
            lax.dynamic_slice(wide_t, (1 - yhi, 0, core * units, 0), (1, 2, units, wide_t.shape[3]))[0],
            lax.dynamic_slice(down, (1 - yhi, core * units, 0), (1, units, down.shape[2])),
        ],
        0,
    )
    theirs, _ = lax.optimization_barrier((theirs, other_kv))
    got_1 = swap(theirs, "yhi")
    got_2 = swap(got_1, "core")
    mine_gu = lax.dynamic_index_in_dim(wide_t, yhi, 0, False)
    mine_d = lax.dynamic_index_in_dim(down, yhi, 0, False)

    axes = [("z", n_z), ("yhi", 2), ("core", n_core), ("cx", n_cx)]
    start = doc_starts(doc_ids, axes) - (ctx - 1) * (2 * half)
    first = yhi * half + z * tok
    info = jnp.stack([first, yhi * half, start[0], start[tok - 1]]).astype(jnp.int32)

    hot_1, w_1 = routing(route_ids, route_weights, yhi, capacity)
    hot_2, w_2 = routing(route_ids, route_weights, 1 - yhi, capacity)
    place = jnp.concatenate([hot_1, hot_2], 1).T

    stream, panels = attend(
        info, queries, hidden_in, start[:, None], norm_gain[None], place, prior_a, prior_b, own_a, own_b
    )
    keep, send = panels[:capacity], panels[capacity:]
    other = swap(send, "yhi")
    rows_a = lax.all_gather(keep, "z", axis=0, tiled=True)
    rows_b = lax.all_gather(other, "z", axis=0, tiled=True)
    out_a = experts(rows_a, mine_gu, mine_d, got_1, got_2)
    out_b = experts(rows_b, mine_gu, mine_d, got_1, got_2)
    sum_a = lax.psum_scatter(out_a, "z", scatter_dimension=0, tiled=True)
    sum_b = lax.psum_scatter(out_b, "z", scatter_dimension=0, tiled=True)
    back = swap(sum_b, "yhi")
    return combine(stream, sum_a, back, hot_1, hot_2, w_1, w_2)


def solution(mesh):
    sizes = {"cx": mesh.shape["ctx"] // 2, "core": 2, "yhi": 2, "z": mesh.shape["exp"] // 2, "dp": mesh.shape["dp"]}
    fine = Mesh(mesh.devices.reshape(tuple(sizes.values())), tuple(sizes))
    tokens = ("dp", "cx", "core", "yhi", "z")
    rows = P(tokens, None)
    hidden = ("yhi", "z")
    in_specs = (rows, rows, rows, P(tokens), rows, rows, P(), P(None, None, None, hidden), P(None, hidden, None))
    return jax.shard_map(
        functools.partial(body, sizes), mesh=fine, in_specs=in_specs, out_specs=rows, check_vma=False
    )
```

time: 661 us -> 338 us (0.51)
  waiting for transfers between devices: 455 us -> 238 us
  matrix products: 66.7 us -> 0 us
  other arithmetic: 46.4 us -> 5.77 us
  Pallas kernels: 0 us -> 39 us
  blocking collectives: 38.2 us -> 0 us
  starting transfers between devices: 4.08 us -> 28 us
  local copies, waits for them, and re-layouts: 36.3 us -> 14 us
    reduce_scatter x1 -> x2, waiting for transfers between devices: 221 us -> 72.3 us  [the longest x1 38 us: body(): sum_a = lax.psum_scatter(out_a, 'z', scatter_dimension=0, tiled=True)]
    all_gather x2 -> x4, waiting for transfers between devices: 232 us -> 98.6 us  [the longest x1 39.1 us: body(): own_b = lax.all_gather(other_kv, 'z', axis=0, tiled=True)]
    dot_general x14 -> x0, matrix products: 66.7 us -> none  [the longest x5 26.6 us: one_span(): jnp.einsum('kgts,skd->kgtd', powers.astype(jnp.bfloat16), value_rows, pre...]
    ppermute x2 -> x14, waiting for transfers between devices: 2.59 us -> 66.1 us  [the longest x5 53 us: shift(): lax.ppermute(value, axis, [(i, (i + steps) % size) for i in range(size)])]
    pallas_call x0 -> x4, Pallas kernels: none -> 39 us  [the longest x1 19.3 us: attend(): pl.pallas_call(functools.partial(attend_kernel, tok=tok, span=span), grid...]
    all_gather x1 -> x0, blocking collectives: 38.2 us -> none  [body(): lax.all_gather(doc_ids, 'exp', axis=0, tiled=True)]
    ppermute x2 -> x14, starting transfers between devices: 3.82 us -> 27.8 us  [the longest x7 14.1 us: doc_starts(): lax.ppermute(counts, axis, [(i, i ^ hop) for i in range(size)])]
    reduce_sum x7 -> x3, other arithmetic: 25.8 us -> 2.29 us  [the longest x1 0.82 us: doc_starts(): return jnp.sum(jnp.where(hot, counts[:1], 0.0), axis=1).astype(jnp.int32)]
  transfers between devices with their start and end apart: 5 -> 20, of which waited for: 4 -> 16; matrix products, arithmetic and copies ran while one was open for 1% -> 4% of each run, Pallas kernels for 0% -> 5%
where the time goes in v1:
time: 338 us
  waiting for transfers between devices  238 us (70%)
  Pallas kernels  39 us (12%)
  starting transfers between devices  28 us (8%)
  local copies, waits for them, and re-layouts  14 us (4%)
  between operations  13.7 us (4%)
  other arithmetic  5.77 us (2%)
    ppermute x5, waiting for transfers between devices, shift(): lax.ppermute(value, axis, [(i, (i + steps) % size) for i in range(size)])  53 us
    all_gather x1, waiting for transfers between devices, body(): own_b = lax.all_gather(other_kv, 'z', axis=0, tiled=True)  39.1 us
    reduce_scatter x1, waiting for transfers between devices, body(): sum_a = lax.psum_scatter(out_a, 'z', scatter_dimension=0, tiled=True)  38 us
    reduce_scatter x1, waiting for transfers between devices, body(): sum_b = lax.psum_scatter(out_b, 'z', scatter_dimension=0, tiled=True)  34.3 us
    all_gather x1, waiting for transfers between devices, body(): rows_a = lax.all_gather(keep, 'z', axis=0, tiled=True)  31.5 us
    all_gather x1, waiting for transfers between devices, body(): own_a = lax.all_gather(keys_values, 'z', axis=0, tiled=True)  28.1 us
    pallas_call x1, Pallas kernels, attend(): pl.pallas_call(functools.partial(attend_kernel, tok=tok, span=span), grid...  19.3 us
    pallas_call x2, Pallas kernels, experts(): pl.pallas_call(expert_kernel, in_specs=[vm, hbm, hbm, hbm, hbm], out_spec...  15.6 us
  transfers between devices with their start and end apart: 20, of which 16 were waited for; matrix products, arithmetic and copies ran while one was open for 4% of the time, Pallas kernels for 5%

profile of v1, /device:TPU:4, one launch (start us, length us, event | category | flops | bytes accessed | tf_op | source)
XLA Modules:
  0.0 338.3 jit_solution(12303770490471299167)
XLA Ops:
  7.3 3.3 collective-permute-start.8
  10.6 6.6 %collective-permute-done.8 = bf16[128,1024]{1,0:T(8,128)(2,1)S(1)} collective-permute-done((bf16[128,1024]{1,0:T(8,128)(2,1)}, bf16[128,1024]{1,0:T(8,128)(2,1)S(1)}, u32[]{:S(2)}, u32[]{:S(2)}) %collective-permute-start.8) | collective-permute-done | bytes 262176 | tf_op jit(solution)/shard_map/ppermute | solution.py:220
  18.7 2.0 collective-permute-start
  22.4 3.3 collective-permute-start.1
  25.7 28.1 %all-gather.5.cloned.1.call-done.oa_ref = bf16[1024,1024]{1,0:T(8,128)(2,1)} async-done(((bf16[128,1024]{1,0:T(8,128)(2,1)}), bf16[1024,1024]{1,0:T(8,128)(2,1)}) %all-gather.5.cloned.1.call-update) | async-done | bytes 2097168 | tf_op jit(solution)/shard_map/all_gather | solution.py:261
  53.7 1.9 collective-permute-start.7
  55.6 39.1 %all-gather.7.cloned.1.call-done.ob_ref = bf16[1024,1024]{1,0:T(8,128)(2,1)} async-done(((bf16[128,1024]{1,0:T(8,128)(2,1)}), bf16[1024,1024]{1,0:T(8,128)(2,1)}) %all-gather.7.cloned.1.call-update) | async-done | bytes 2097168 | tf_op jit(solution)/shard_map/all_gather | solution.py:262
  94.7 1.9 collective-permute-start.9
  96.7 3.2 collective-permute-start.2
  100.2 4.1 %collective-permute-done.2 = f32[8,128]{1,0:T(8,128)S(1)} collective-permute-done((f32[8,128]{1,0:T(8,128)S(1)}, f32[8,128]{1,0:T(8,128)S(1)}, u32[]{:S(2)}, u32[]{:S(2)}) %collective-permute-start.2) | collective-permute-done | bytes 4128 | tf_op jit(solution)/shard_map/ppermute | solution.py:234
  104.3 3.0 collective-permute-start.3
  107.7 1.7 collective-permute-done.3
  111.9 2.3 collective-permute-done.5
  114.2 1.4 collective-permute-start.6
  116.5 2.9 collective-permute-done.6
  121.0 1.3 pad_add_fusion.info_ref
  122.5 1.2 copy-done.2
  123.6 1.2 copy-done.3
  124.8 19.3 %attend.1 = (bf16[128,3584]{1,0:T(8,128)(2,1)S(1)}, bf16[64,3584]{1,0:T(8,128)(2,1)S(1)}) custom-call(s32[4]{0:T(128)S(1)} %pad_add_fusion.info_ref, bf16[128,3584]{1,0:T(8,128)(2,1)S(1)} %copy-done.2, bf16[128,3584]{1,0:T(8,128)(2,1)S(1)} %copy-done.3, s32[128,1]{1,0:T(8,128)S(1)} %copy.24.start_ref, bf16[1,3584]{1,0:T(2,128)(2,1)S(1)} %broadcast_in_dim.50.gain_ref, ...), custom_call_target="tpu_custom_call" | custom-call | flops 4000000000 | bytes 12582912 | tf_op jit(solution)/shard_map/attend/pallas_call | solution.py:139
  145.8 7.5 %collective-permute-done.12 = bf16[32,3584]{1,0:T(8,128)(2,1)S(1)} collective-permute-done((bf16[32,3584]{1,0:T(8,128)(2,1)S(1)}, bf16[32,3584]{1,0:T(8,128)(2,1)S(1)}, u32[]{:S(2)}, u32[]{:S(2)}) %collective-permute-start.12) | collective-permute-done | bytes 229408 | tf_op jit(solution)/shard_map/ppermute | solution.py:220
  154.2 1.3 dynamic-slice_bitcast_fusion.1
  155.5 1.3 pad_maximum_fusion
  157.0 38.5 %collective-permute-done.10.r1_ref = bf16[3,80,3584]{2,1,0:T(8,128)(2,1)} collective-permute-done((bf16[3,80,3584]{2,1,0:T(8,128)(2,1)}, bf16[3,80,3584]{2,1,0:T(8,128)(2,1)}, u32[]{:S(2)}, u32[]{:S(2)}) %collective-permute-start.10) | collective-permute-done | bytes 1720352 | tf_op jit(solution)/shard_map/ppermute | solution.py:220
  195.5 3.5 %collective-permute-start.11 = (bf16[3,80,3584]{2,1,0:T(8,128)(2,1)}, bf16[3,80,3584]{2,1,0:T(8,128)(2,1)}, u32[]{:S(2)}, u32[]{:S(2)}) collective-permute-start(bf16[3,80,3584]{2,1,0:T(8,128)(2,1)} %collective-permute-done.10.r1_ref), channel_id=1, source_target_pairs={{0,32},{32,0},{1,33},{33,1},{2,34},{34,2},{3,35},{35,3},{4,36},{36... | collective-permute-start | bytes 5160968 | tf_op jit(solution)/shard_map/ppermute | solution.py:220
  199.0 3.2 dynamic-slice_bitcast_fusion.wo_ref
  202.5 7.8 %experts.3 = bf16[256,3584]{1,0:T(8,128)(2,1)} custom-call(bf16[256,3584]{1,0:T(8,128)(2,1)} %all-gather.11.cloned.1.call-done.x_ref, bf16[2,160,3584]{2,1,0:T(8,128)(2,1)} %dynamic-slice_bitcast_fusion.wo_ref, bf16[160,3584]{1,0:T(8,128)(2,1)S(1)} %dynamic-slice_bitcast_fusion.2.do_ref, bf16[3,80,3584]{2,1,0:T(8,128)(2,1)} %collective-permute-done.10.r1_ref, ...), custom_call_target="tpu_custom_call" | custom-call | flops 1761607680 | bytes 10551296 | tf_op jit(solution)/shard_map/experts/pallas_call | solution.py:185
  210.4 31.5 %all-gather.9.cloned.1.call-done.x_ref = bf16[256,3584]{1,0:T(8,128)(2,1)} async-done(((bf16[32,3584]{1,0:T(8,128)(2,1)}), bf16[256,3584]{1,0:T(8,128)(2,1)}) %all-gather.9.cloned.1.call-update) | async-done | bytes 1835024 | tf_op jit(solution)/shard_map/all_gather | solution.py:296
  241.9 7.8 %experts.2 = bf16[256,3584]{1,0:T(8,128)(2,1)} custom-call(bf16[256,3584]{1,0:T(8,128)(2,1)} %all-gather.9.cloned.1.call-done.x_ref, bf16[2,160,3584]{2,1,0:T(8,128)(2,1)} %dynamic-slice_bitcast_fusion.wo_ref, bf16[160,3584]{1,0:T(8,128)(2,1)S(1)} %dynamic-slice_bitcast_fusion.2.do_ref, bf16[3,80,3584]{2,1,0:T(8,128)(2,1)} %collective-permute-done.10.r1_ref, ...), custom_call_target="tpu_custom_call" | custom-call | flops 1761607680 | bytes 10551296 | tf_op jit(solution)/shard_map/experts/pallas_call | solution.py:185
  249.7 34.3 %reduce-scatter.5.cloned.1.call-done = bf16[32,3584]{1,0:T(8,128)(2,1)} async-done(((bf16[256,3584]{1,0:T(8,128)(2,1)}), bf16[32,3584]{1,0:T(8,128)(2,1)}) %reduce-scatter.5.cloned.1.call-update) | async-done | bytes 229392 | tf_op jit(solution)/shard_map/reduce_scatter | solution.py:301
  284.0 3.2 collective-permute-start.13
  288.6 38.0 %reduce-scatter.3.cloned.1.call-done.keep_ref = bf16[32,3584]{1,0:T(8,128)(2,1)} async-done(((bf16[256,3584]{1,0:T(8,128)(2,1)}), bf16[32,3584]{1,0:T(8,128)(2,1)}) %reduce-scatter.3.cloned.1.call-update) | async-done | bytes 229392 | tf_op jit(solution)/shard_map/reduce_scatter | solution.py:300
  327.4 4.0 %combine.1 = bf16[128,3584]{1,0:T(8,128)(2,1)} custom-call(bf16[128,3584]{1,0:T(8,128)(2,1)} %copy-done.1, bf16[32,3584]{1,0:T(8,128)(2,1)} %reduce-scatter.3.cloned.1.call-done.keep_ref, bf16[32,3584]{1,0:T(8,128)(2,1)} %copy-done.7, bf16[128,32]{1,0:T(8,128)(2,1)} %copy-done.4, bf16[128,32]{1,0:T(8,128)(2,1)} %copy-done.5, f32[128,1]{1,0:T(8,128)} %copy.26.w1_ref, ...), custom_call_target="tpu_custom_call" | custom-call | tf_op jit(solution)/shard_map/combine/pallas_call | solution.py:209
  (76 shorter events, 14.9 us)
Async XLA Ops:
  6.5 147.6 %copy-start = (bf16[2,160,3584]{2,1,0:T(8,128)(2,1)S(1)}, bf16[2,160,3584]{2,1,0:T(8,128)(2,1)}, u32[]{:S(2)}) copy-start(bf16[2,160,3584]{2,1,0:T(8,128)(2,1)} %param.17) | copy-start | bytes 6881284
  6.5 47.2 %all-gather.5.cloned.1.call-start = ((), (), s32[]{:S(2)}) async-start(), calls=%async_computation.2 | async-start | bytes 2359296 | tf_op jit(solution)/shard_map/all_gather | solution.py:261
  7.3 87.5 %all-gather.7.cloned.1.call-start = ((), (), s32[]{:S(2)}) async-start(), calls=%async_computation.3 | async-start | bytes 2359296 | tf_op jit(solution)/shard_map/all_gather | solution.py:262
  7.3 9.8 %collective-permute-start.8 = (bf16[128,1024]{1,0:T(8,128)(2,1)}, bf16[128,1024]{1,0:T(8,128)(2,1)S(1)}, u32[]{:S(2)}, u32[]{:S(2)}) collective-permute-start(bf16[128,1024]{1,0:T(8,128)(2,1)} %param.11), channel_id=1, source_target_pairs={{0,16},{16,0},{1,17},{17,1},{2,18},{18,2},{3,19},{19,3},{4,20},{20... | collective-permute-start | bytes 786440 | tf_op jit(solution)/shard_map/ppermute | solution.py:220
  17.2 0.7 copy-start.6
  17.9 184.7 %all-gather.11.cloned.1.call-start = ((), (), s32[]{:S(2)}) async-start(), calls=%async_computation.6 | async-start | bytes 2064384 | tf_op jit(solution)/shard_map/all_gather | solution.py:297
  18.7 3.7 %collective-permute-start = (f32[8,128]{1,0:T(8,128)S(1)}, f32[8,128]{1,0:T(8,128)S(1)}, u32[]{:S(2)}, u32[]{:S(2)}) collective-permute-start(f32[8,128]{1,0:T(8,128)S(1)} %broadcast_in_dim.28), channel_id=1, source_target_pairs={{0,2},{2,0},{4,6},{6,4},{8,10},{10,8},{12,14},{14,12},{1,3},{3,1},... | collective-permute-start | bytes 12296 | tf_op jit(solution)/shard_map/ppermute | solution.py:234
  22.4 74.3 %collective-permute-start.1 = (f32[8,128]{1,0:T(8,128)S(1)}, f32[8,128]{1,0:T(8,128)S(1)}, u32[]{:S(2)}, u32[]{:S(2)}) collective-permute-start(f32[8,128]{1,0:T(8,128)S(1)} %broadcast_add_fusion), channel_id=1, source_target_pairs={{0,4},{2,6},{4,0},{6,2},{8,12},{10,14},{12,8},{14,10},{1,5},{3,7},... | collective-permute-start | bytes 12296 | tf_op jit(solution)/shard_map/ppermute | solution.py:234
  53.7 68.6 %collective-permute-start.7 = (bf16[1024,1024]{1,0:T(8,128)(2,1)}, bf16[1024,1024]{1,0:T(8,128)(2,1)}, u32[]{:S(2)}, u32[]{:S(2)}) collective-permute-start(bf16[1024,1024]{1,0:T(8,128)(2,1)} %all-gather.5.cloned.1.call-done.oa_ref), channel_id=1, source_target_pairs={{0,32},{32,64},{64,96},{96,128},{128,160},{160,192},{192,224},{1,3... | collective-permute-start | bytes 6291464 | tf_op jit(solution)/shard_map/ppermute | solution.py:264
  94.7 27.7 %collective-permute-start.9 = (bf16[1024,1024]{1,0:T(8,128)(2,1)}, bf16[1024,1024]{1,0:T(8,128)(2,1)}, u32[]{:S(2)}, u32[]{:S(2)}) collective-permute-start(bf16[1024,1024]{1,0:T(8,128)(2,1)} %all-gather.7.cloned.1.call-done.ob_ref), channel_id=1, source_target_pairs={{0,32},{32,64},{64,96},{96,128},{128,160},{160,192},{192,224},{1,3... | collective-permute-start | bytes 6291464 | tf_op jit(solution)/shard_map/ppermute | solution.py:265
  96.7 7.6 %collective-permute-start.2 = (f32[8,128]{1,0:T(8,128)S(1)}, f32[8,128]{1,0:T(8,128)S(1)}, u32[]{:S(2)}, u32[]{:S(2)}) collective-permute-start(f32[8,128]{1,0:T(8,128)S(1)} %fusion.7), channel_id=1, source_target_pairs={{0,8},{2,10},{4,12},{6,14},{8,0},{10,2},{12,4},{14,6},{1,9},{3,11}... | collective-permute-start | bytes 12296 | tf_op jit(solution)/shard_map/ppermute | solution.py:234
  104.3 5.1 %collective-permute-start.3 = (f32[8,128]{1,0:T(8,128)S(1)}, f32[8,128]{1,0:T(8,128)S(1)}, u32[]{:S(2)}, u32[]{:S(2)}) collective-permute-start(f32[8,128]{1,0:T(8,128)S(1)} %add.62), channel_id=1, source_target_pairs={{0,16},{16,0},{1,17},{17,1},{2,18},{18,2},{3,19},{19,3},{4,20},{20... | collective-permute-start | bytes 12296 | tf_op jit(solution)/shard_map/ppermute | solution.py:234
  109.4 1.2 collective-permute-start.4
  110.6 3.6 %collective-permute-start.5 = (f32[8,128]{1,0:T(8,128)S(1)}, f32[8,128]{1,0:T(8,128)S(1)}, u32[]{:S(2)}, u32[]{:S(2)}) collective-permute-start(f32[8,128]{1,0:T(8,128)S(1)} %add.64), channel_id=1, source_target_pairs={{0,64},{64,0},{128,192},{192,128},{1,65},{65,1},{129,193},{193,129... | collective-permute-start | bytes 12296 | tf_op jit(solution)/shard_map/ppermute | solution.py:234
  111.9 32.2 %copy-start.4 = (bf16[128,32]{1,0:T(8,128)(2,1)}, bf16[128,32]{1,0:T(8,128)(2,1)S(1)}, u32[]{:S(2)}) copy-start(bf16[128,32]{1,0:T(8,128)(2,1)S(1)} %get-tuple-element.21.hot1_ref) | copy-start | bytes 24580
  111.9 32.2 %copy-start.5 = (bf16[128,32]{1,0:T(8,128)(2,1)}, bf16[128,32]{1,0:T(8,128)(2,1)S(1)}, u32[]{:S(2)}) copy-start(bf16[128,32]{1,0:T(8,128)(2,1)S(1)} %get-tuple-element.22.hot2_ref) | copy-start | bytes 24580
  114.2 5.2 %collective-permute-start.6 = (f32[8,128]{1,0:T(8,128)S(1)}, f32[8,128]{1,0:T(8,128)S(1)}, u32[]{:S(2)}, u32[]{:S(2)}) collective-permute-start(f32[8,128]{1,0:T(8,128)S(1)} %add.65), channel_id=1, source_target_pairs={{0,128},{64,192},{128,0},{192,64},{1,129},{65,193},{129,1},{193,65... | collective-permute-start | bytes 12296 | tf_op jit(solution)/shard_map/ppermute | solution.py:234
  122.4 1.2 copy-start.2
  123.6 1.2 copy-start.3
  144.2 0.9 copy-start.1
  145.8 7.5 %collective-permute-start.12 = (bf16[32,3584]{1,0:T(8,128)(2,1)S(1)}, bf16[32,3584]{1,0:T(8,128)(2,1)S(1)}, u32[]{:S(2)}, u32[]{:S(2)}) collective-permute-start(bf16[32,3584]{1,0:T(8,128)(2,1)S(1)} %get-tuple-element.15), channel_id=1, source_target_pairs={{0,16},{16,0},{1,17},{17,1},{2,18},{18,2},{3,19},{19,3},{4,20},{20... | collective-permute-start | bytes 688136 | tf_op jit(solution)/shard_map/ppermute | solution.py:220
  153.4 0.7 copy-start.8
  154.1 87.8 %all-gather.9.cloned.1.call-start = ((), (), s32[]{:S(2)}) async-start(), calls=%async_computation.4 | async-start | bytes 2064384 | tf_op jit(solution)/shard_map/all_gather | solution.py:296
  156.9 38.6 %collective-permute-start.10 = (bf16[3,80,3584]{2,1,0:T(8,128)(2,1)}, bf16[3,80,3584]{2,1,0:T(8,128)(2,1)}, u32[]{:S(2)}, u32[]{:S(2)}) collective-permute-start(bf16[3,80,3584]{2,1,0:T(8,128)(2,1)} %pad_maximum_fusion), channel_id=1, source_target_pairs={{0,16},{16,0},{1,17},{17,1},{2,18},{18,2},{3,19},{19,3},{4,20},{20... | collective-permute-start | bytes 5160968 | tf_op jit(solution)/shard_map/ppermute | solution.py:220
  156.9 127.1 %reduce-scatter.5.cloned.1.call-start = ((), (), s32[]{:S(2)}) async-start(), calls=%async_computation.7 | async-start | bytes 2064384 | tf_op jit(solution)/shard_map/reduce_scatter | solution.py:301
  195.5 7.0 %collective-permute-start.11 = (bf16[3,80,3584]{2,1,0:T(8,128)(2,1)}, bf16[3,80,3584]{2,1,0:T(8,128)(2,1)}, u32[]{:S(2)}, u32[]{:S(2)}) collective-permute-start(bf16[3,80,3584]{2,1,0:T(8,128)(2,1)} %collective-permute-done.10.r1_ref), channel_id=1, source_target_pairs={{0,32},{32,0},{1,33},{33,1},{2,34},{34,2},{3,35},{35,3},{4,36},{36... | collective-permute-start | bytes 5160968 | tf_op jit(solution)/shard_map/ppermute | solution.py:220
  210.4 116.3 %reduce-scatter.3.cloned.1.call-start = ((), (), s32[]{:S(2)}) async-start(), calls=%async_computation.5 | async-start | bytes 2064384 | tf_op jit(solution)/shard_map/reduce_scatter | solution.py:300
  284.0 42.7 %collective-permute-start.13 = (bf16[32,3584]{1,0:T(8,128)(2,1)}, bf16[32,3584]{1,0:T(8,128)(2,1)S(1)}, u32[]{:S(2)}, u32[]{:S(2)}) collective-permute-start(bf16[32,3584]{1,0:T(8,128)(2,1)} %reduce-scatter.5.cloned.1.call-done), channel_id=1, source_target_pairs={{0,16},{16,0},{1,17},{17,1},{2,18},{18,2},{3,19},{19,3},{4,20},{20... | collective-permute-start | bytes 688136 | tf_op jit(solution)/shard_map/ppermute | solution.py:220
  326.7 0.7 copy-start.7
Sparse Core Ops, SparseCore 0:
  9.1 44.5 all-gather.4
  55.5 39.1 all-gather.6
  154.2 46.2 all-gather.10
  202.2 39.6 all-gather.8
  244.3 39.6 reduce-scatter.4
  286.4 40.2 reduce-scatter.2
